TPU v7x, 256 devices: a whole 4x4x8 slice. The times are simulated.
256 devices in a mesh: cam: 8 (over x, y_lo), tok: 32 (over z, y_hi, core).
Axes of the slice: x: 4, y: 4 (y_hi: 2, y_lo: 2; y = y_hi * 2 + y_lo), z: 8, core: 2. Of those that a mesh axis runs over, the one named last changes fastest.
Arguments:
- camera_q: bfloat16 [8, 32768, 1536], P('cam', 'tok'), may hold values from -6 to 6
- camera_v: bfloat16 [8, 32768, 1536], P('cam', 'tok'), may hold values from -6 to 6
- lidar_k: bfloat16 [1024, 1536], P('tok'), may hold values from -6 to 6
- lidar_v: bfloat16 [1024, 1536], P('tok'), may hold values from -6 to 6
- head_bias: float32 [12], replicated, may hold values from -2 to 0
Outputs:
- camera_out: bfloat16 [8, 32768, 1536], P('cam', 'tok')
- lidar_out: bfloat16 [1024, 1536], P('tok')
All inputs are finite; a program needn't handle non-finite values.
Results may differ from a plain program's by a relative error of at most 0.005.
Values may be sent and summed in bfloat16 or wider, within the bound.
A program may use at most 192 MiB of HBM per device.

v0:
```python
import functools

import jax
import jax.numpy as jnp
from jax import lax
from jax.experimental import pallas as pl
from jax.experimental.pallas import tpu as pltpu
from jax.sharding import PartitionSpec as P

HEADS = 12
HEAD_DIM = 128
WIDTH = HEADS * HEAD_DIM
SLOTS = 8
OFFSETS = (0, 1, -1, 2, -2, 3, -3, 4)
GROUPS = ((0, 1), (1, 2), (3, 2), (5, 2), (7, 1))
ROWS = 32
XCOLS = 384
F32, BF16 = jnp.float32, jnp.bfloat16


def kernel(
    q_hbm, cv_hbm, k_hbm, v_hbm, bias, co, lo,
    q, cv, kb, vb, u_all, pb, crecv, psend, precv, zkeep, zsend, zrecv, lob,
    load_sem, k_send, k_recv, ks_send, ks_recv, v_send, v_recv,
    c_send, c_recv, p_send, p_recv, z_send, z_recv, l_send, l_recv,
):
    cam, tok = lax.axis_index("cam"), lax.axis_index("tok")
    x, y_lo = cam // 2, cam % 2
    z, y_hi, core = tok // 4, (tok // 2) % 2, tok % 2
    y = y_hi * 2 + y_lo

    def device(dx, dy, dz):
        xx, yy, zz = (x + dx + 4) % 4, (y + dy + 4) % 4, (z + dz + 8) % 8
        return (xx * 2 + yy % 2, zz * 4 + (yy // 2) * 2 + core)

    sibling = (cam, z * 4 + y_hi * 2 + (1 - core))
    mirror = (x * 2 + (1 - y_lo), z * 4 + (1 - y_hi) * 2 + core)
    up, down = device(0, 0, 1), device(0, 0, -1)
    in_plane = [(dx, dy) for dx in range(4) for dy in range(4) if dx + dy > 0]

    my_rows = pl.ds(pl.multiple_of(y_lo * 16, 16), 16)
    my_cols = pl.ds(pl.multiple_of(x * XCOLS, XCOLS), XCOLS)

    loads = [
        pltpu.make_async_copy(k_hbm, kb.at[0, y_hi, core], load_sem.at[0]),
        pltpu.make_async_copy(v_hbm.at[my_rows, my_cols], vb.at[0, y_hi, core, my_rows, my_cols], load_sem.at[1]),
        pltpu.make_async_copy(q_hbm, q, load_sem.at[2]),
        pltpu.make_async_copy(cv_hbm, cv, load_sem.at[3]),
    ]
    for copy in loads:
        copy.start()

    barrier = pltpu.get_barrier_semaphore()
    partners = [sibling] + [device(dx, dy, 0) for dx, dy in in_plane] + [device(0, 0, dz) for dz in range(1, 8)]
    for partner in partners:
        pl.semaphore_signal(barrier, inc=1, device_id=partner, device_id_type=pl.DeviceIdType.MESH)
    pl.semaphore_wait(barrier, len(partners))

    drains = []

    def send(src, dst, send_sem, recv_sem, to):
        copy = pltpu.make_async_remote_copy(
            src_ref=src, dst_ref=dst, send_sem=send_sem, recv_sem=recv_sem,
            device_id=to, device_id_type=pl.DeviceIdType.MESH,
        )
        copy.start()
        return copy

    def half(p):
        return y_hi if p == 0 else 1 - y_hi

    class Ring:
        def __init__(self, buf, send_sem, recv_sem, s_send, s_recv):
            self.buf, self.send_sem, self.recv_sem = buf, send_sem, recv_sem
            self.s_send, self.s_recv = s_send, s_recv

        def block(self, slot, p):
            return self.buf.at[slot, half(p), core]

        def hop(self, slot, p, to, into):
            copy = send(self.block(slot, p), self.block(into, p), self.send_sem.at[into, p], self.recv_sem.at[into, p], to)
            drains.append(copy)

        def share(self, slot, p):
            block = self.block(slot, p)
            drains.append(send(block, block, self.s_send.at[slot, p], self.s_recv.at[slot, p], sibling))

        def near(self):
            block = self.block(0, 0)
            drains.append(send(block, block, self.send_sem.at[0, 0], self.recv_sem.at[0, 1], mirror))
            self.share(0, 0)

        def begin(self, p):
            self.hop(0, p, down, 1)
            self.hop(0, p, up, 2)

        def arrive(self, slot, p):
            block = self.block(slot, p)
            pltpu.make_async_copy(block, block, self.recv_sem.at[slot, p]).wait()
            if slot == 0:
                self.begin(p)
            elif slot in (1, 3) or (slot == 5 and p == 0):
                self.hop(slot, p, down, slot + 2)
            elif slot in (2, 4) or (slot == 6 and p == 1):
                self.hop(slot, p, up, slot + 2 if slot < 6 else 7)
            self.share(slot, p)

        def shared(self, slot):
            for p in range(2):
                block = self.buf.at[slot, half(p), 1 - core]
                pltpu.make_async_copy(block, block, self.s_recv.at[slot, p]).wait()

    keys = Ring(kb, k_send, k_recv, ks_send, ks_recv)

    near, far = pl.ds(0, 4), pl.ds(4, 4)

    def done(ref, sem):
        pltpu.make_async_copy(ref, ref, sem).wait()

    from_z = vb.at[pl.ds(1, 7), y_hi, core, my_rows, my_cols]
    near_piece = vb.at[near, y_hi, core, my_rows, my_cols]
    far_piece = vb.at[far, y_hi, core, my_rows, my_cols]
    near_row = vb.at[near, y_hi, core, my_rows]
    far_column = vb.at[far, :, core, :, my_cols]
    three_pieces = vb.at[near, y_hi, core, my_rows, pl.ds(0, 3 * XCOLS)]
    three_columns = vb.at[far, :, core, :, pl.ds(0, 3 * XCOLS)]

    def values_z():
        piece = vb.at[0, y_hi, core, my_rows, my_cols]
        for s in range(1, SLOTS):
            send(piece, vb.at[s, y_hi, core, my_rows, my_cols], v_send.at[0], v_recv.at[0], device(0, 0, -OFFSETS[s]))

    def values_first():
        done(from_z, v_recv.at[0])
        for d in range(1, 4):
            send(near_piece, near_piece, v_send.at[1], v_recv.at[1], device(d, 0, 0))
            send(far_piece, far_piece, v_send.at[2], v_recv.at[2], device(0, d, 0))

    def values_second():
        done(three_pieces, v_recv.at[1])
        done(three_pieces, v_recv.at[2])
        for d in range(1, 4):
            send(near_row, near_row, v_send.at[6 + d], v_recv.at[3 + d], device(0, d, 0))
            send(far_column, far_column, v_send.at[4], v_recv.at[3], device(d, 0, 0))

    def values_share():
        for d in range(1, 4):
            done(near_row, v_recv.at[3 + d])
        done(three_columns, v_recv.at[3])
        for i, slots in enumerate((near, far)):
            send(vb.at[slots, :, core], vb.at[slots, :, core], v_send.at[5 + i], v_recv.at[7 + i], sibling)

    def values_shared():
        for i, slots in enumerate((near, far)):
            done(vb.at[slots, :, 1 - core], v_recv.at[7 + i])

    def values_sent():
        done(from_z, v_send.at[0])
        done(three_pieces, v_send.at[1])
        done(three_pieces, v_send.at[2])
        for d in range(3):
            done(near_row, v_send.at[7 + d])
        done(three_columns, v_send.at[4])
        for i, slots in enumerate((near, far)):
            done(vb.at[slots, :, core], v_send.at[5 + i])

    def head(h):
        return pl.ds(h * HEAD_DIM if isinstance(h, int) else pl.multiple_of(h * HEAD_DIM, HEAD_DIM), HEAD_DIM)

    def attend(group, first, count):
        slot, ns = GROUPS[group]
        rows = ns * 128

        for h in range(first, first + count):
            key = kb[slot : slot + ns, :, :, :, head(h)].reshape(rows, HEAD_DIM)
            s = lax.dot_general(key, q[:, head(h)], (((1,), (1,)), ((), ())), preferred_element_type=F32)
            u = (jnp.tanh(s * (0.5 / HEAD_DIM**0.5) + bias[h] * 0.5) + 1.0).astype(BF16)
            u_all[h, slot * 128 : slot * 128 + rows, :] = u
            part = jnp.dot(u, cv[:, head(h)], preferred_element_type=F32)
            pb[slot : slot + ns, :, :, :, head(h)] = part.astype(BF16).reshape(ns, 2, 2, ROWS, HEAD_DIM)

    def core_send(group):
        slot, ns = GROUPS[group]
        src = pb.at[pl.ds(slot, ns), :, 1 - core]
        drains.append(send(src, crecv.at[pl.ds(slot, ns)], c_send.at[group], c_recv.at[group], sibling))

    def plane_send(group):
        slot, ns = GROUPS[group]
        block = crecv.at[pl.ds(slot, ns)]
        pltpu.make_async_copy(block, block, c_recv.at[group]).wait()
        for s in range(slot, slot + ns):
            for hi in range(2):
                total = pb[s, hi, core].astype(F32) + crecv[s, hi].astype(F32)
                psend[s, hi] = total.astype(BF16)
        for dx, dy in in_plane:
            xx, yy = (x + dx) % 4, (y + dy) % 4
            rows = pl.ds(pl.multiple_of((yy % 2) * 16, 16), 16)
            cols = pl.ds(pl.multiple_of(xx * XCOLS, XCOLS), XCOLS)
            src = psend.at[pl.ds(slot, ns), yy // 2, rows, cols]
            send(src, precv.at[dx * 4 + dy, pl.ds(slot, ns)], p_send.at[group], p_recv.at[group], device(dx, dy, 0))

    def plane_sum(group):
        slot, ns = GROUPS[group]
        block = precv.at[pl.ds(1, 15), pl.ds(slot, ns)]
        pltpu.make_async_copy(block, block, p_recv.at[group]).wait()
        rows = pl.ds(pl.multiple_of(y_lo * 16, 16), 16)
        cols = pl.ds(pl.multiple_of(x * XCOLS, XCOLS), XCOLS)
        for s in range(slot, slot + ns):
            total = psend[s, y_hi, rows, cols].astype(F32)
            for i in range(1, 16):
                total = total + precv[i, s].astype(F32)
            if s == 0:
                zkeep[...] = total
            else:
                zsend[s] = total.astype(BF16)
                send(zsend.at[s], zrecv.at[s], z_send, z_recv, device(0, 0, OFFSETS[s]))

    def finish():
        block = zrecv.at[pl.ds(1, 7)]
        pltpu.make_async_copy(block, block, z_recv).wait()
        total = zkeep[...]
        for s in range(1, SLOTS):
            total = total + zrecv[s].astype(F32)
        rows = pl.ds(pl.multiple_of(y_lo * 16, 16), 16)
        cols = pl.ds(pl.multiple_of(x * XCOLS, XCOLS), XCOLS)
        lob[rows, cols] = (total * (1.0 / 1024.0)).astype(BF16)
        mine = lob.at[rows, cols]
        for dx in range(4):
            for dl in range(2):
                if dx + dl > 0:
                    to = (((x + dx) % 4) * 2 + (y_lo + dl) % 2, tok)
                    send(mine, mine, l_send, l_recv, to)

    def camera(first, count, unroll):
        def body(i, carry):
            for j in range(unroll):
                h = first + i * unroll + j
                value = vb[:, :, :, :, head(h)].reshape(SLOTS * 128, HEAD_DIM)
                out = jnp.dot(value.T, u_all[h], preferred_element_type=F32)
                co[:, head(h)] = (out * (1.0 / 64.0)).astype(BF16).T
            return carry

        lax.fori_loop(0, count // unroll, body, 0)

    loads[0].wait()
    keys.near()
    keys.begin(0)
    loads[1].wait()
    values_z()
    keys.arrive(0, 1)
    keys.arrive(1, 0)
    keys.arrive(2, 0)
    loads[2].wait()
    loads[3].wait()
    keys.shared(0)
    values_first()
    attend(0, 0, 6)
    keys.arrive(1, 1)
    keys.arrive(2, 1)
    attend(0, 6, 6)
    core_send(0)
    keys.arrive(3, 0)
    keys.arrive(4, 0)
    keys.shared(1)
    keys.shared(2)
    attend(1, 0, 6)
    keys.arrive(3, 1)
    keys.arrive(4, 1)
    values_second()
    plane_send(0)
    attend(1, 6, 6)
    core_send(1)
    keys.arrive(5, 0)
    keys.arrive(6, 0)
    keys.shared(3)
    keys.shared(4)
    attend(2, 0, 6)
    keys.arrive(5, 1)
    keys.arrive(6, 1)
    plane_send(1)
    attend(2, 6, 6)
    core_send(2)
    keys.arrive(7, 0)
    keys.shared(5)
    keys.shared(6)
    attend(3, 0, 6)
    keys.arrive(7, 1)
    plane_send(2)
    plane_sum(0)
    attend(3, 6, 6)
    core_send(3)
    keys.shared(7)
    attend(4, 0, 6)
    plane_send(3)
    plane_sum(1)
    attend(4, 6, 6)
    core_send(4)
    values_share()
    plane_send(4)
    plane_sum(2)
    plane_sum(3)
    values_shared()
    plane_sum(4)
    camera(0, 6, 2)
    finish()
    camera(6, 6, 2)

    block = precv.at[pl.ds(0, 7), 0]
    pltpu.make_async_copy(block, block, l_recv).wait()
    lo[...] = lob[...]
    for copy in drains:
        copy.wait_send()
    values_sent()
    for group, (slot, ns) in enumerate(GROUPS):
        block = precv.at[pl.ds(1, 15), pl.ds(slot, ns)]
        pltpu.make_async_copy(block, block, p_send.at[group]).wait()
    block = zsend.at[pl.ds(1, 7)]
    pltpu.make_async_copy(block, block, z_send).wait()
    block = precv.at[pl.ds(0, 7), 0]
    pltpu.make_async_copy(block, block, l_send).wait()


def shards(camera_q, camera_v, lidar_k, lidar_v, head_bias):
    tokens = camera_q.shape[1]
    hbm = pl.BlockSpec(memory_space=pl.ANY)
    dma = pltpu.SemaphoreType.DMA
    planes = (SLOTS, 2, 2, ROWS, WIDTH)
    camera_out, lidar_out = pl.pallas_call(
        kernel,
        out_shape=[
            pltpu.VMEM((tokens, WIDTH), BF16),
            pltpu.VMEM((ROWS, WIDTH), BF16),
        ],
        in_specs=[hbm, hbm, hbm, hbm, pl.BlockSpec(memory_space=pltpu.SMEM)],
        out_specs=[pl.BlockSpec(memory_space=pltpu.VMEM)] * 2,
        scratch_shapes=[
            pltpu.VMEM((tokens, WIDTH), BF16),
            pltpu.VMEM((tokens, WIDTH), BF16),
            pltpu.VMEM(planes, BF16),
            pltpu.VMEM(planes, BF16),
            pltpu.VMEM((HEADS, SLOTS * 128, tokens), BF16),
            pltpu.VMEM(planes, BF16),
            pltpu.VMEM((SLOTS, 2, ROWS, WIDTH), BF16),
            pltpu.VMEM((SLOTS, 2, ROWS, WIDTH), BF16),
            pltpu.VMEM((16, SLOTS, 16, XCOLS), BF16),
            pltpu.VMEM((16, XCOLS), F32),
            pltpu.VMEM((SLOTS, 16, XCOLS), BF16),
            pltpu.VMEM((SLOTS, 16, XCOLS), BF16),
            pltpu.VMEM((ROWS, WIDTH), BF16),
            dma((4,)),
            dma((SLOTS, 2)), dma((SLOTS, 2)), dma((SLOTS, 2)), dma((SLOTS, 2)),
            dma((10,)), dma((9,)),
            dma((5,)), dma((5,)), dma((5,)), dma((5,)),
            dma, dma, dma, dma,
        ],
        compiler_params=pltpu.CompilerParams(
            collective_id=0, has_side_effects=True, vmem_limit_bytes=54 << 20
        ),
        name="fused",
    )(camera_q.reshape(tokens, WIDTH), camera_v.reshape(tokens, WIDTH), lidar_k, lidar_v, head_bias)
    return camera_out.reshape(camera_q.shape), lidar_out


def solution(mesh):
    return jax.shard_map(
        shards,
        mesh=mesh,
        in_specs=(
            P("cam", "tok", None),
            P("cam", "tok", None),
            P("tok", None),
            P("tok", None),
            P(),
        ),
        out_specs=(P("cam", "tok", None), P("tok", None)),
        check_vma=False,
    )
```

profile of v0, /device:TPU:1, one launch (start us, length us, event | category | flops | bytes accessed | tf_op | source)
XLA Modules:
  0.0 67.7 jit_solution(9147849022461844960)
XLA Ops:
  0.6 64.8 %fused.1 = (bf16[1024,1536]{1,0:T(8,128)(2,1)S(1)}, bf16[32,1536]{1,0:T(8,128)(2,1)S(1)}) custom-call(bf16[1024,1536]{1,0:T(8,128)(2,1)} %bitcast.4, bf16[1024,1536]{1,0:T(8,128)(2,1)} %bitcast.5, bf16[32,1536]{1,0:T(8,128)(2,1)} %k_hbm.1, bf16[32,1536]{1,0:T(8,128)(2,1)} %v_hbm.1, f32[12]{0:T(128)} %bias.1), custom_call_target="tpu_custom_call" | custom-call | tf_op jit(solution)/shard_map/fused/pallas_call | solution.py:328
  65.4 1.7 %copy.9 = bf16[1,1024,1536]{2,1,0:T(8,128)(2,1)} copy(bf16[1,1024,1536]{2,1,0:T(8,128)(2,1)S(1)} %bitcast.3) | data formatting | bytes 6291456
  67.1 0.6 copy.10
where the time goes:
time: 69 us; the launch traced here: 67.7 us
  Pallas kernels  64.8 us (94%)
  local copies, waits for them, and re-layouts  2.31 us (3%)
    pallas_call x1, Pallas kernels, shards(): pl.pallas_call(kernel, out_shape=[pltpu.VMEM((tokens, WIDTH), BF16), pltp...  64.8 us
    unnamed x2, local copies, waits for them, and re-layouts  2.31 us

commit v1 on v0

--- a/solution.py
+++ b/solution.py
@@ -21,7 +21,7 @@
 def kernel(
     q_hbm, cv_hbm, k_hbm, v_hbm, bias, co, lo,
     q, cv, kb, vb, u_all, pb, crecv, psend, precv, zkeep, zsend, zrecv, lob,
-    load_sem, k_send, k_recv, ks_send, ks_recv, v_send, v_recv,
+    load_sem, k_send, k_recv, ks_send, ks_recv, v_send, v_recv, w_send, w_recv, ws_send, ws_recv,
     c_send, c_recv, p_send, p_recv, z_send, z_recv, l_send, l_recv,
 ):
     cam, tok = lax.axis_index("cam"), lax.axis_index("tok")
@@ -43,7 +43,7 @@
 
     loads = [
         pltpu.make_async_copy(k_hbm, kb.at[0, y_hi, core], load_sem.at[0]),
-        pltpu.make_async_copy(v_hbm.at[my_rows, my_cols], vb.at[0, y_hi, core, my_rows, my_cols], load_sem.at[1]),
+        pltpu.make_async_copy(v_hbm, vb.at[0, y_hi, core], load_sem.at[1]),
         pltpu.make_async_copy(q_hbm, q, load_sem.at[2]),
         pltpu.make_async_copy(cv_hbm, cv, load_sem.at[3]),
     ]
@@ -70,7 +70,8 @@
         return y_hi if p == 0 else 1 - y_hi
 
     class Ring:
-        def __init__(self, buf, send_sem, recv_sem, s_send, s_recv):
+        def __init__(self, buf, send_sem, recv_sem, s_send, s_recv, onward):
+            self.onward = onward
             self.buf, self.send_sem, self.recv_sem = buf, send_sem, recv_sem
             self.s_send, self.s_recv = s_send, s_recv
 
@@ -99,6 +100,8 @@
             pltpu.make_async_copy(block, block, self.recv_sem.at[slot, p]).wait()
             if slot == 0:
                 self.begin(p)
+            elif not self.onward:
+                pass
             elif slot in (1, 3) or (slot == 5 and p == 0):
                 self.hop(slot, p, down, slot + 2)
             elif slot in (2, 4) or (slot == 6 and p == 1):
@@ -110,24 +113,26 @@
                 block = self.buf.at[slot, half(p), 1 - core]
                 pltpu.make_async_copy(block, block, self.s_recv.at[slot, p]).wait()
 
-    keys = Ring(kb, k_send, k_recv, ks_send, ks_recv)
-
-    near, far = pl.ds(0, 4), pl.ds(4, 4)
+    keys = Ring(kb, k_send, k_recv, ks_send, ks_recv, True)
+    values = Ring(vb, w_send, w_recv, ws_send, ws_recv, False)
+
+    near, far = pl.ds(3, 2), pl.ds(5, 3)
 
     def done(ref, sem):
         pltpu.make_async_copy(ref, ref, sem).wait()
 
-    from_z = vb.at[pl.ds(1, 7), y_hi, core, my_rows, my_cols]
+    from_z = vb.at[pl.ds(3, 5), y_hi, core, my_rows, my_cols]
     near_piece = vb.at[near, y_hi, core, my_rows, my_cols]
     far_piece = vb.at[far, y_hi, core, my_rows, my_cols]
     near_row = vb.at[near, y_hi, core, my_rows]
     far_column = vb.at[far, :, core, :, my_cols]
-    three_pieces = vb.at[near, y_hi, core, my_rows, pl.ds(0, 3 * XCOLS)]
+    three_near = vb.at[near, y_hi, core, my_rows, pl.ds(0, 3 * XCOLS)]
+    three_far = vb.at[far, y_hi, core, my_rows, pl.ds(0, 3 * XCOLS)]
     three_columns = vb.at[far, :, core, :, pl.ds(0, 3 * XCOLS)]
 
     def values_z():
         piece = vb.at[0, y_hi, core, my_rows, my_cols]
-        for s in range(1, SLOTS):
+        for s in range(3, SLOTS):
             send(piece, vb.at[s, y_hi, core, my_rows, my_cols], v_send.at[0], v_recv.at[0], device(0, 0, -OFFSETS[s]))
 
     def values_first():
@@ -137,8 +142,8 @@
             send(far_piece, far_piece, v_send.at[2], v_recv.at[2], device(0, d, 0))
 
     def values_second():
-        done(three_pieces, v_recv.at[1])
-        done(three_pieces, v_recv.at[2])
+        done(three_near, v_recv.at[1])
+        done(three_far, v_recv.at[2])
         for d in range(1, 4):
             send(near_row, near_row, v_send.at[6 + d], v_recv.at[3 + d], device(0, d, 0))
             send(far_column, far_column, v_send.at[4], v_recv.at[3], device(d, 0, 0))
@@ -156,8 +161,8 @@
 
     def values_sent():
         done(from_z, v_send.at[0])
-        done(three_pieces, v_send.at[1])
-        done(three_pieces, v_send.at[2])
+        done(three_near, v_send.at[1])
+        done(three_far, v_send.at[2])
         for d in range(3):
             done(near_row, v_send.at[7 + d])
         done(three_columns, v_send.at[4])
@@ -248,6 +253,7 @@
     loads[1].wait()
     values_z()
     keys.arrive(0, 1)
+    values.near()
     keys.arrive(1, 0)
     keys.arrive(2, 0)
     loads[2].wait()
@@ -277,6 +283,8 @@
     attend(2, 0, 6)
     keys.arrive(5, 1)
     keys.arrive(6, 1)
+    values.begin(0)
+    values.arrive(0, 1)
     plane_send(1)
     attend(2, 6, 6)
     core_send(2)
@@ -295,12 +303,17 @@
     plane_sum(1)
     attend(4, 6, 6)
     core_send(4)
+    for s in range(1, 3):
+        for p in range(2):
+            values.arrive(s, p)
+    plane_sum(2)
+    plane_send(4)
     values_share()
-    plane_send(4)
-    plane_sum(2)
     plane_sum(3)
+    plane_sum(4)
+    for s in range(3):
+        values.shared(s)
     values_shared()
-    plane_sum(4)
     camera(0, 6, 2)
     finish()
     camera(6, 6, 2)
@@ -350,6 +363,7 @@
             dma((4,)),
             dma((SLOTS, 2)), dma((SLOTS, 2)), dma((SLOTS, 2)), dma((SLOTS, 2)),
             dma((10,)), dma((9,)),
+            dma((3, 2)), dma((3, 2)), dma((3, 2)), dma((3, 2)),
             dma((5,)), dma((5,)), dma((5,)), dma((5,)),
             dma, dma, dma, dma,
         ],

time: 69 us -> 64.3 us (0.932); the launches traced: 67.7 us -> 64.2 us
  Pallas kernels: 64.8 us -> 61.2 us
    pallas_call x1, Pallas kernels: 64.8 us -> 61.2 us  [shards(): pl.pallas_call(kernel, out_shape=[pltpu.VMEM((tokens, WIDTH), BF16), pltp...]
where the time goes in v1:
time: 64.3 us; the launch traced here: 64.2 us
  Pallas kernels  61.2 us (95%)
  local copies, waits for them, and re-layouts  2.31 us (4%)
    pallas_call x1, Pallas kernels, shards(): pl.pallas_call(kernel, out_shape=[pltpu.VMEM((tokens, WIDTH), BF16), pltp...  61.2 us
    unnamed x2, local copies, waits for them, and re-layouts  2.31 us

profile of v1, /device:TPU:1, one launch (start us, length us, event | category | flops | bytes accessed | tf_op | source)
XLA Modules:
  0.0 64.2 jit_solution(4131483589604152466)
XLA Ops:
  0.6 61.2 %fused.1 = (bf16[1024,1536]{1,0:T(8,128)(2,1)S(1)}, bf16[32,1536]{1,0:T(8,128)(2,1)S(1)}) custom-call(bf16[1024,1536]{1,0:T(8,128)(2,1)} %bitcast.4, bf16[1024,1536]{1,0:T(8,128)(2,1)} %bitcast.5, bf16[32,1536]{1,0:T(8,128)(2,1)} %k_hbm.1, bf16[32,1536]{1,0:T(8,128)(2,1)} %v_hbm.1, f32[12]{0:T(128)} %bias.1), custom_call_target="tpu_custom_call" | custom-call | tf_op jit(solution)/shard_map/fused/pallas_call | solution.py:341
  61.9 1.7 %copy.9 = bf16[1,1024,1536]{2,1,0:T(8,128)(2,1)} copy(bf16[1,1024,1536]{2,1,0:T(8,128)(2,1)S(1)} %bitcast.3) | data formatting | bytes 6291456
  63.5 0.6 copy.10

commit v2 on v1

--- a/solution.py
+++ b/solution.py
@@ -303,11 +303,11 @@
     plane_sum(1)
     attend(4, 6, 6)
     core_send(4)
+    plane_send(4)
     for s in range(1, 3):
         for p in range(2):
             values.arrive(s, p)
     plane_sum(2)
-    plane_send(4)
     values_share()
     plane_sum(3)
     plane_sum(4)

time: 64.3 us -> 64.2 us (level)
  no operation moved by 1% of the time
where the time goes in v2:
time: 64.2 us; the launch traced here: 64.1 us
  Pallas kernels  61.1 us (95%)
  local copies, waits for them, and re-layouts  2.31 us (4%)
    pallas_call x1, Pallas kernels, shards(): pl.pallas_call(kernel, out_shape=[pltpu.VMEM((tokens, WIDTH), BF16), pltp...  61.1 us
    unnamed x2, local copies, waits for them, and re-layouts  2.31 us

profile of v2, /device:TPU:1, one launch (start us, length us, event | category | flops | bytes accessed | tf_op | source)
XLA Modules:
  0.0 64.1 jit_solution(15420619975640056826)
XLA Ops:
  0.6 61.1 %fused.1 = (bf16[1024,1536]{1,0:T(8,128)(2,1)S(1)}, bf16[32,1536]{1,0:T(8,128)(2,1)S(1)}) custom-call(bf16[1024,1536]{1,0:T(8,128)(2,1)} %bitcast.4, bf16[1024,1536]{1,0:T(8,128)(2,1)} %bitcast.5, bf16[32,1536]{1,0:T(8,128)(2,1)} %k_hbm.1, bf16[32,1536]{1,0:T(8,128)(2,1)} %v_hbm.1, f32[12]{0:T(128)} %bias.1), custom_call_target="tpu_custom_call" | custom-call | tf_op jit(solution)/shard_map/fused/pallas_call | solution.py:341
  61.8 1.7 %copy.9 = bf16[1,1024,1536]{2,1,0:T(8,128)(2,1)} copy(bf16[1,1024,1536]{2,1,0:T(8,128)(2,1)S(1)} %bitcast.3) | data formatting | bytes 6291456
  63.4 0.6 copy.10
